TPU v7x, 256 devices: a whole 4x4x8 slice. The times are simulated.
256 devices in a mesh: dp: 16 (over z_hi, x, core), slot: 4 (over y), hid: 4 (over z_lo).
Axes of the slice: x: 4, y: 4, z: 8 (z_hi: 2, z_lo: 4; z = z_hi * 4 + z_lo), core: 2. Of those that a mesh axis runs over, the one named last changes fastest.
Arguments:
- master_weights: float32 [8, 3, 768, 2048], P('slot', None, 'hid', 'dp'), may hold values from -0.125 to 0.125
- first_moment: float32 [8, 3, 768, 2048], P('slot', None, 'hid', 'dp'), may hold values from -6 to 6
- second_moment: float32 [8, 3, 768, 2048], P('slot', None, 'hid', 'dp'), may hold values from 1 to 100
- tokens_one: bfloat16 [16384, 2048], P('dp'), may hold values from -6 to 6
- grad_out: bfloat16 [16384, 2048], P('dp'), may hold values from -6 to 6
- route_one: int32 [16384, 2], P('dp'), may hold values from 0 to 7, all different within a row
- prob_one: float32 [16384, 2], P('dp'), may hold values from 0.05 to 0.6
- tokens_two: bfloat16 [16384, 2048], P('dp'), may hold values from -6 to 6
- route_two: int32 [16384, 2], P('dp'), may hold values from 0 to 7, all different within a row
- prob_two: float32 [16384, 2], P('dp'), may hold values from 0.05 to 0.6
- old_order: int32 [8], replicated, may hold values from 0 to 7, each once
- new_order: int32 [8], replicated, may hold values from 0 to 7, each once
Outputs:
- moved_master: float32 [8, 3, 768, 2048], P('slot', None, 'hid', 'dp')
- moved_first: float32 [8, 3, 768, 2048], P('slot', None, 'hid', 'dp')
- moved_second: float32 [8, 3, 768, 2048], P('slot', None, 'hid', 'dp')
- next_output: bfloat16 [16384, 2048], P('dp', ('slot', 'hid'))
Inputs may be any that keep to these rules, and one draw needn't show every extreme that they name: `old_order`: lists each of the 8 experts once. `new_order`: lists each of the 8 experts once. `route_one`: each row names 2 different experts. `route_two`: each row names 2 different experts.
All inputs are finite; a program needn't handle non-finite values.
Results may differ from a plain program's by a relative error of at most 0.017.
Values may be sent and summed in bfloat16 or wider, within the bound.
No kernel may reach another device: no remote copies, remote signals or barrier semaphores. Data moves between devices by JAX's collectives and lax.ppermute only.
A program may use at most 128 MiB of HBM per device.

v0:
```python
import jax
import jax.numpy as jnp
from jax import lax
from jax.sharding import Mesh
from jax.sharding import PartitionSpec as P

DP = ("dp_0", "dp_1", "dp_2")
learn_rate = 0.001
beta_one = 0.9
beta_two = 0.95
epsilon = 1e-08
decay_rate = 0.1


def in_blocks(x, dim, size):
    before, after = (x.shape[:dim], x.shape[dim + 1 :])
    return jnp.moveaxis(x.reshape(*before, size, -1, *after), dim, 0)


def summed_rows(x, chips, core, dim):
    sizes = (lax.axis_size(chips), lax.axis_size(core))
    pieces = in_blocks(x, dim, sizes[0] * sizes[1])
    inside = pieces.shape[1:]
    pieces = pieces.reshape(*sizes, *inside).swapaxes(0, 1).reshape(-1, *inside)
    pieces = lax.psum_scatter(pieces, core, scatter_dimension=0, tiled=True)
    return lax.psum_scatter(pieces, chips, scatter_dimension=0, tiled=True)[0]


def scatter_axes(x, axes, dim):
    if not axes:
        return x
    nearer = lax.psum_scatter(x, axes[0], scatter_dimension=dim, tiled=True)
    return scatter_axes(nearer, axes[1:], dim)


def rows_by(left, right):
    return lax.dot_general(
        left, right, (((1,), (1,)), ((), ())), preferred_element_type=jnp.float32
    )


def cols_by(left, right):
    return lax.dot_general(
        left, right, (((0,), (0,)), ((), ())), preferred_element_type=jnp.float32
    )


def expert_parts(tokens, grad_out, scaling, weights):
    gate_proj = rows_by(tokens, weights[0])
    up_proj = rows_by(tokens, weights[1])
    logistic = jax.nn.sigmoid(gate_proj)
    swish_gate = gate_proj * logistic
    activated = (swish_gate * up_proj).astype(jnp.bfloat16)
    scaled_grad = (scaling[:, None] * grad_out.astype(jnp.float32)).astype(jnp.bfloat16)
    d_activated = rows_by(scaled_grad, weights[2])
    d_gate = (d_activated * up_proj * logistic * (1.0 + gate_proj * (1.0 - logistic))).astype(
        jnp.bfloat16
    )
    d_up = (d_activated * swish_gate).astype(jnp.bfloat16)
    return (d_gate, d_up, activated, scaled_grad)


def expert_out(tokens, scaling, weights):
    gate_proj = rows_by(tokens, weights[0])
    up_proj = rows_by(tokens, weights[1])
    mixed = (scaling[:, None] * gate_proj * jax.nn.sigmoid(gate_proj) * up_proj).astype(
        jnp.bfloat16
    )
    return jnp.dot(mixed, weights[2], preferred_element_type=jnp.float32)


def adamw_update(master, moment_a, moment_b, grad_sum):
    new_a = beta_one * moment_a + (1.0 - beta_one) * grad_sum
    new_b = beta_two * moment_b + (1.0 - beta_two) * grad_sum * grad_sum
    fixed_a = new_a / (1.0 - beta_one**10)
    fixed_b = new_b / (1.0 - beta_two**10)
    new_master = master - learn_rate * (
        fixed_a / (jnp.sqrt(fixed_b) + epsilon) + decay_rate * master
    )
    return (new_master, new_a, new_b)


def coefficients(routes, probs, expert_ids):
    matches = routes[:, :, None] == expert_ids[None, None, :]
    return jnp.sum(jnp.where(matches, probs[:, :, None], 0.0), axis=1)


def per_device(
    master_weights,
    first_moment,
    second_moment,
    tokens_one,
    grad_out,
    route_one,
    prob_one,
    tokens_two,
    route_two,
    prob_two,
    old_order,
    new_order,
):
    local_count = master_weights.shape[0]
    slot_index = lax.axis_index("slot")
    slot_count = lax.axis_size("slot")
    offset = slot_index * local_count
    held_ids = lax.dynamic_slice_in_dim(old_order, offset, local_count)
    shard_weights = master_weights.astype(jnp.bfloat16)
    full_weights = lax.all_gather(shard_weights, DP, axis=3, tiled=True)
    scaling_one = coefficients(route_one, prob_one, held_ids)
    parts = [
        expert_parts(tokens_one, grad_out, scaling_one[:, expert], full_weights[expert])
        for expert in range(local_count)
    ]
    gradients = jnp.stack(
        [
            jnp.stack(
                [
                    cols_by(part[0], tokens_one),
                    cols_by(part[1], tokens_one),
                    cols_by(part[2], part[3]),
                ]
            )
            for part in parts
        ]
    )
    owned_grads = summed_rows(gradients.astype(jnp.bfloat16), ("dp_0", "dp_1"), "dp_2", 3).astype(
        jnp.float32
    )
    new_master, new_a, new_b = adamw_update(
        master_weights, first_moment, second_moment, owned_grads
    )
    positions = jnp.arange(old_order.shape[0], dtype=jnp.int32)
    source = jnp.sum(
        jnp.where(old_order[None, :] == new_order[:, None], positions[None, :], 0), axis=1
    )
    owner_slot = source // local_count
    within = source % local_count
    my_owners = lax.dynamic_slice_in_dim(owner_slot, offset, local_count)
    pick_rows = my_owners * local_count + jnp.arange(local_count, dtype=jnp.int32)

    def outgoing(state_block):
        picked = jnp.take(state_block, within, axis=0)
        return picked.reshape((slot_count, local_count) + state_block.shape[1:])

    arrived = (
        lax.all_to_all(outgoing(new_master), "slot", split_axis=0, concat_axis=0, tiled=True),
        lax.all_to_all(outgoing(new_a), "slot", split_axis=0, concat_axis=0, tiled=True),
        lax.all_to_all(outgoing(new_b), "slot", split_axis=0, concat_axis=0, tiled=True),
    )
    moved_states = tuple(
        (
            jnp.take(
                state_block.reshape((slot_count * local_count,) + state_block.shape[2:]),
                pick_rows,
                axis=0,
            )
            for state_block in arrived
        )
    )
    moved_master, moved_first, moved_second = moved_states
    next_shard = new_master.astype(jnp.bfloat16)
    next_full = lax.all_gather(next_shard, DP, axis=3, tiled=True)
    scaling_two = coefficients(route_two, prob_two, held_ids)
    partial_value = expert_out(tokens_two, scaling_two[:, 0], next_full[0])
    expert = 1
    partial_value = partial_value + expert_out(
        tokens_two, scaling_two[:, expert], next_full[expert]
    )
    mixed_out = scatter_axes(partial_value, ("slot", "hid"), 1).astype(jnp.bfloat16)
    return (moved_master, moved_first, moved_second, mixed_out)


def solution(mesh):
    split = Mesh(
        mesh.devices.reshape(2, 4, 2, mesh.shape["slot"], mesh.shape["hid"]),
        ("dp_0", "dp_1", "dp_2", "slot", "hid"),
    )
    in_specs = (
        P("slot", None, "hid", DP),
        P("slot", None, "hid", DP),
        P("slot", None, "hid", DP),
        P(DP, None),
        P(DP, None),
        P(DP, None),
        P(DP, None),
        P(DP, None),
        P(DP, None),
        P(DP, None),
        P(),
        P(),
    )
    out_specs = (
        P("slot", None, "hid", DP),
        P("slot", None, "hid", DP),
        P("slot", None, "hid", DP),
        P(DP, ("slot", "hid")),
    )
    return jax.shard_map(
        per_device, mesh=split, in_specs=in_specs, out_specs=out_specs, check_vma=False
    )
```

profile of v0, /device:TPU:2, one launch (start us, length us, event | category | flops | bytes accessed | tf_op | source)
XLA Modules:
  0.0 531.8 jit_solution(10620187443816465604)
XLA Ops:
  7.2 1.8 convert_element_type.53
  9.1 0.7 dynamic_slice.6
  9.8 0.8 fusion.54
  10.7 85.3 %all-gather.3.cloned.1.call-done = bf16[2,3,192,2048]{3,2,1,0:T(8,128)(2,1)} async-done(((bf16[2,3,192,128]{3,2,1,0:T(8,128)(2,1)}), bf16[2,3,192,2048]{3,2,1,0:T(8,128)(2,1)}) %all-gather.3.cloned.1.call-update) | async-done | bytes 4718608 | tf_op jit(solution)/shard_map/all_gather | solution.py:108
  96.0 4.1 fusion.24
  100.1 3.9 fusion.23
  104.0 1.3 fusion.15
  105.3 1.6 fusion.3
  107.0 0.5 copy-done.6
  107.5 1.1 fusion.14
  108.6 1.2 fusion.13
  109.8 1.5 fusion.26
  111.4 1.5 fusion.25
  112.9 1.3 fusion.10
  114.2 1.6 fusion.6
  115.8 1.1 fusion.9
  116.9 1.4 fusion.8
  118.4 0.2 copy.31
  118.6 0.2 copy.30
  118.8 0.2 copy.29
  118.9 0.2 copy.28
  119.1 0.2 copy.27
  119.3 0.6 maximum_maximum_fusion
  119.9 3.4 copy.26
  123.3 14.0 %reduce-scatter.5.cloned.1.call-done = bf16[8,2,3,192,128]{4,3,2,1,0:T(8,128)(2,1)} async-done(((bf16[16,2,3,192,128]{4,3,2,1,0:T(8,128)(2,1)}), bf16[8,2,3,192,128]{4,3,2,1,0:T(8,128)(2,1)}) %reduce-scatter.5.cloned.1.call-update) | async-done | bytes 2359312 | tf_op jit(solution)/shard_map/reduce_scatter | solution.py:25
  137.4 105.3 %reduce-scatter.7.cloned.1.call-done = bf16[1,2,3,192,128]{4,3,2,1,0:T(8,128)(2,1)} async-done(((bf16[8,2,3,192,128]{4,3,2,1,0:T(8,128)(2,1)}), bf16[1,2,3,192,128]{4,3,2,1,0:T(8,128)(2,1)}) %reduce-scatter.7.cloned.1.call-update) | async-done | bytes 294928 | tf_op jit(solution)/shard_map/reduce_scatter | solution.py:26
  242.7 2.2 fusion.63
  244.9 78.6 %all-gather.5.cloned.1.call-done = bf16[2,3,192,2048]{3,2,1,0:T(8,128)(2,1)} async-done(((bf16[2,3,192,128]{3,2,1,0:T(8,128)(2,1)}), bf16[2,3,192,2048]{3,2,1,0:T(8,128)(2,1)}) %all-gather.5.cloned.1.call-update) | async-done | bytes 4718608 | tf_op jit(solution)/shard_map/all_gather | solution.py:162
  323.5 4.1 fusion.22
  327.7 2.7 fusion.21
  330.3 8.6 %fusion.19 = f32[1024,2048]{1,0:T(8,128)} fusion(bf16[1024,2048]{1,0:T(8,128)(2,1)} %param.23, bf16[2,3,192,2048]{3,2,1,0:T(8,128)(2,1)} %all-gather.5.cloned.1.call-done, f32[192,1024]{1,0:T(8,128)S(1)} %fusion.22, f32[1024]{0:T(1024)S(1)} %bitcast.109), kind=kOutput, calls=%fused_computation.29 | convolution fusion | flops 1611988992 | bytes 14946304 | tf_op jit(solution)/shard_map/dot_general | solution.py:69
  338.9 11.1 %convolution_add_fusion = f32[1024,2048]{1,0:T(8,128)} fusion(f32[1024,2048]{1,0:T(8,128)} %fusion.19, bf16[1024,2048]{1,0:T(8,128)(2,1)} %param.23, bf16[2,3,192,2048]{3,2,1,0:T(8,128)(2,1)} %all-gather.5.cloned.1.call-done, f32[192,1024]{1,0:T(8,128)S(1)} %fusion.21, f32[1024]{0:T(1024)S(1)} %bitcast.108), kind=kOutput, calls=%fused_computation.11 | convolution fusion | flops 1614086144 | bytes 23334912 | tf_op jit(solution)/shard_map/dot_general | solution.py:69
  350.1 0.6 copy-done.7
  350.7 0.2 select_reduce_fusion
  350.9 2.1 gather_fusion.4
  353.0 2.2 gather_fusion.2
  355.2 2.2 gather_fusion
  357.3 6.7 %broadcast_select_fusion = (f32[8,3,192,128]{3,2,1,0:T(8,128)}, f32[8,3,192,128]{3,2,1,0:T(8,128)S(1)}, f32[8,3,192,128]{3,2,1,0:T(8,128)}) fusion(f32[8,3,192,128]{3,2,1,0:T(8,128)} %gather_fusion.4, pred[8]{0:T(512)(128)(4,1)S(1)} %get-tuple-element.14, f32[8,3,192,128]{3,2,1,0:T(8,128)} %gather_fusion.2, f32[8,3,192,128]{3,2,1,0:T(8,128)} %gather_fusion), kind=kLoop, calls=%fused_computation.31 | loop fusion | flops 1769472 | bytes 14155784 | tf_op jit(solution)/shard_map/jit(_take)/select_n | solution.py:142
  364.0 4.5 all-to-all-start.2
  368.6 85.9 %reduce-scatter.9.cloned.1.call-done = f32[1024,512]{1,0:T(8,128)} async-done(((f32[1024,2048]{1,0:T(8,128)}), f32[1024,512]{1,0:T(8,128)}) %reduce-scatter.9.cloned.1.call-update) | async-done | bytes 2097168 | tf_op jit(solution)/shard_map/reduce_scatter | solution.py:32
  454.6 32.7 %all_to_all.15 = f32[4,2,3,192,128]{4,3,2,1,0:T(8,128)} all-to-all(f32[4,2,3,192,128]{4,3,2,1,0:T(8,128)S(1)} %bitcast.98), channel_id=1, replica_groups=mesh['dp_0'=2,'dp_1'=4,'dp_2'=2,'slot'=4,'hid'=4] {'slot'}, dimensions={0} | all-to-all | bytes 4718592 | tf_op jit(solution)/shard_map/all_to_all | solution.py:147
  487.3 3.6 all-to-all-start
  491.1 2.2 gather_fusion.5
  493.3 2.2 gather_fusion.3
  495.6 23.8 %all-to-all-done = f32[4,2,3,192,128]{4,3,2,1,0:T(8,128)S(1)} async-done(((f32[4,2,3,192,128]{4,3,2,1,0:T(8,128)}), f32[4,2,3,192,128]{4,3,2,1,0:T(8,128)S(1)}, u32[]{:S(2)}, u32[]{:S(2)}) %all-to-all-start) | async-done | bytes 2359328 | tf_op jit(solution)/shard_map/all_to_all | solution.py:146
  519.4 1.4 gather_fusion.1
  520.8 2.4 broadcast_select_fusion.3
  523.1 1.8 convert_element_type.66
  (37 shorter events, 0.7 us)
Async XLA Ops:
  7.2 88.8 %all-gather.3.cloned.1.call-start = ((), (), s32[]{:S(2)}) async-start(), calls=%async_computation.7 | async-start | bytes 5013504 | tf_op jit(solution)/shard_map/all_gather | solution.py:108
  9.1 128.2 %reduce-scatter.5.cloned.1.call-start = ((), (), s32[]{:S(2)}) async-start(), calls=%async_computation.8 | async-start | bytes 7077888 | tf_op jit(solution)/shard_map/reduce_scatter | solution.py:25
  96.0 4.1 copy-start.4
  100.1 3.9 copy-start.5
  105.3 2.2 copy-start.6
  123.2 119.5 %copy-start.1 = (f32[2,3,192,128]{3,2,1,0:T(8,128)S(1)}, f32[2,3,192,128]{3,2,1,0:T(8,128)}, u32[]{:S(2)}) copy-start(f32[2,3,192,128]{3,2,1,0:T(8,128)} %param.16) | copy-start | bytes 1769476
  123.2 119.5 %copy-start.2 = (f32[2,3,192,128]{3,2,1,0:T(8,128)S(1)}, f32[2,3,192,128]{3,2,1,0:T(8,128)}, u32[]{:S(2)}) copy-start(f32[2,3,192,128]{3,2,1,0:T(8,128)} %param.17) | copy-start | bytes 1769476
  123.2 119.5 %copy-start.3 = (f32[2,3,192,128]{3,2,1,0:T(8,128)S(1)}, f32[2,3,192,128]{3,2,1,0:T(8,128)}, u32[]{:S(2)}) copy-start(f32[2,3,192,128]{3,2,1,0:T(8,128)} %param.18) | copy-start | bytes 1769476
  123.2 119.4 %reduce-scatter.7.cloned.1.call-start = ((), (), s32[]{:S(2)}) async-start(), calls=%async_computation.9 | async-start | bytes 2654208 | tf_op jit(solution)/shard_map/reduce_scatter | solution.py:26
  137.3 186.2 %all-gather.5.cloned.1.call-start = ((), (), s32[]{:S(2)}) async-start(), calls=%async_computation.10 | async-start | bytes 5013504 | tf_op jit(solution)/shard_map/all_gather | solution.py:162
  244.9 209.7 %reduce-scatter.9.cloned.1.call-start = ((), (), s32[]{:S(2)}) async-start(), calls=%async_computation.11 | async-start | bytes 10485760 | tf_op jit(solution)/shard_map/reduce_scatter | solution.py:32
  323.5 4.1 copy-start
  350.0 0.7 copy-start.7
  350.0 0.7 copy-start.8
  364.0 90.5 %all-to-all-start.2 = ((f32[4,2,3,192,128]{4,3,2,1,0:T(8,128)}), f32[4,2,3,192,128]{4,3,2,1,0:T(8,128)}, u32[]{:S(2)}, u32[]{:S(2)}) async-start(f32[4,2,3,192,128]{4,3,2,1,0:T(8,128)} %bitcast.99), calls=%async_computation.4 | async-start | bytes 4718592 | tf_op jit(solution)/shard_map/all_to_all | solution.py:148
  368.6 154.6 %reduce-scatter.11.cloned.1.call-start = ((), (), s32[]{:S(2)}) async-start(), calls=%async_computation.12 | async-start | bytes 2621440 | tf_op jit(solution)/shard_map/reduce_scatter | solution.py:32
  487.3 32.1 %all-to-all-start = ((f32[4,2,3,192,128]{4,3,2,1,0:T(8,128)}), f32[4,2,3,192,128]{4,3,2,1,0:T(8,128)S(1)}, u32[]{:S(2)}, u32[]{:S(2)}) async-start(f32[4,2,3,192,128]{4,3,2,1,0:T(8,128)} %bitcast.14), calls=%async_computation.2 | async-start | bytes 4718592 | tf_op jit(solution)/shard_map/all_to_all | solution.py:146
Sparse Core Ops, SparseCore 0:
  11.1 84.8 all-gather.2
  123.4 13.8 reduce-scatter.4
  142.0 100.6 reduce-scatter.6
  245.7 77.8 all-gather.4
  350.2 104.3 reduce-scatter.8
  456.9 48.0 reduce-scatter.10
where the time goes:
time: 532 us
  waiting for transfers between devices  393 us (74%)
  matrix products  48.1 us (9%)
  blocking collectives  32.7 us (6%)
  local copies, waits for them, and re-layouts  18.6 us (3%)
  other arithmetic  16.6 us (3%)
  between operations  14.4 us (3%)
  starting transfers between devices  8.42 us (2%)
    reduce_scatter x1, waiting for transfers between devices, summed_rows(): return lax.psum_scatter(pieces, chips, scatter_dimension=0, tiled=True)[0]  105 us
    reduce_scatter x2, waiting for transfers between devices, scatter_axes(): nearer = lax.psum_scatter(x, axes[0], scatter_dimension=dim, tiled=True)  85.9 us
    all_gather x1, waiting for transfers between devices, per_device(): full_weights = lax.all_gather(shard_weights, DP, axis=3, tiled=True)  85.3 us
    all_gather x1, waiting for transfers between devices, per_device(): next_full = lax.all_gather(next_shard, DP, axis=3, tiled=True)  78.6 us
    all_to_all x1, blocking collectives, per_device(): lax.all_to_all(outgoing(new_a), 'slot', split_axis=0, concat_axis=0, tile...  32.7 us
    all_to_all x1, waiting for transfers between devices, per_device(): lax.all_to_all(outgoing(new_master), 'slot', split_axis=0, concat_axis=0,...  23.8 us
    dot_general x8, matrix products, rows_by(): lax.dot_general(left, right, (((1,), (1,)), ((), ())), preferred_element_...  21.1 us
    dot_general x2, matrix products, expert_out(): return jnp.dot(mixed, weights[2], preferred_element_type=jnp.float32)  19.7 us
  transfers between devices with their start and end apart: 8, of which 6 were waited for; matrix products, arithmetic and copies ran while one was open for 4% of the time, Pallas kernels for 0%

commit v1 on v0

--- a/solution.py
+++ b/solution.py
@@ -10,6 +10,22 @@
 beta_two = 0.95
 epsilon = 1e-08
 decay_rate = 0.1
+
+
+def pairwise_exchange(value, axis, split, join):
+    ways, here = (lax.axis_size(axis), lax.axis_index(axis))
+    width = value.shape[split] // ways
+    lengths = list(value.shape)
+    lengths[split] = width
+    height = lengths[join]
+    lengths[join] = height * ways
+    full = jnp.zeros(lengths, value.dtype)
+    for mask in range(ways):
+        part = lax.dynamic_slice_in_dim(value, (here ^ mask) * width, width, axis=split)
+        if mask:
+            part = lax.ppermute(part, axis, [(d, d ^ mask) for d in range(ways)])
+        full = lax.dynamic_update_slice_in_dim(full, part, (here ^ mask) * height, axis=join)
+    return full
 
 
 def in_blocks(x, dim, size):
@@ -144,7 +160,7 @@
 
     arrived = (
         lax.all_to_all(outgoing(new_master), "slot", split_axis=0, concat_axis=0, tiled=True),
-        lax.all_to_all(outgoing(new_a), "slot", split_axis=0, concat_axis=0, tiled=True),
+        pairwise_exchange(outgoing(new_a), "slot", 0, 0),
         lax.all_to_all(outgoing(new_b), "slot", split_axis=0, concat_axis=0, tiled=True),
     )
     moved_states = tuple(

time: 532 us -> 544 us (1.023)
  waiting for transfers between devices: 393 us -> 400 us
  local copies, waits for them, and re-layouts: 18.6 us -> 24.8 us
    ppermute x0 -> x3, waiting for transfers between devices: none -> 45 us  [pairwise_exchange(): part = lax.ppermute(part, axis, [(d, d ^ mask) for d in range(ways)])]
    all_to_all x1, waiting for transfers between devices: 23.8 us -> 0.01 us  [per_device(): lax.all_to_all(outgoing(new_master), 'slot', split_axis=0, concat_axis=0,...]
    reduce_scatter x2, waiting for transfers between devices: 85.9 us -> 71.9 us  [scatter_axes(): nearer = lax.psum_scatter(x, axes[0], scatter_dimension=dim, tiled=True)]
  transfers between devices with their start and end apart: 8 -> 10, of which waited for: 6 -> 7; matrix products, arithmetic and copies ran while one was open for 4% -> 5% of each run, Pallas kernels for 0% -> 0%
where the time goes in v1:
time: 544 us
  waiting for transfers between devices  400 us (74%)
  matrix products  48.1 us (9%)
  blocking collectives  32.7 us (6%)
  local copies, waits for them, and re-layouts  24.8 us (5%)
  between operations  14.4 us (3%)
  other arithmetic  14.1 us (3%)
  starting transfers between devices  9.66 us (2%)
    reduce_scatter x1, waiting for transfers between devices, summed_rows(): return lax.psum_scatter(pieces, chips, scatter_dimension=0, tiled=True)[0]  105 us
    all_gather x1, waiting for transfers between devices, per_device(): full_weights = lax.all_gather(shard_weights, DP, axis=3, tiled=True)  85.3 us
    all_gather x1, waiting for transfers between devices, per_device(): next_full = lax.all_gather(next_shard, DP, axis=3, tiled=True)  78.6 us
    reduce_scatter x2, waiting for transfers between devices, scatter_axes(): nearer = lax.psum_scatter(x, axes[0], scatter_dimension=dim, tiled=True)  71.9 us
    ppermute x3, waiting for transfers between devices, pairwise_exchange(): part = lax.ppermute(part, axis, [(d, d ^ mask) for d in range(ways)])  45 us
    all_to_all x1, blocking collectives, per_device(): lax.all_to_all(outgoing(new_b), 'slot', split_axis=0, concat_axis=0, tile...  32.7 us
    dot_general x8, matrix products, rows_by(): lax.dot_general(left, right, (((1,), (1,)), ((), ())), preferred_element_...  21.1 us
    dot_general x2, matrix products, expert_out(): return jnp.dot(mixed, weights[2], preferred_element_type=jnp.float32)  19.7 us
  transfers between devices with their start and end apart: 10, of which 7 were waited for; matrix products, arithmetic and copies ran while one was open for 5% of the time, Pallas kernels for 0%

profile of v1, /device:TPU:2, one launch (start us, length us, event | category | flops | bytes accessed | tf_op | source)
XLA Modules:
  0.0 543.9 jit_solution(7674911993912574130)
XLA Ops:
  7.2 1.8 convert_element_type.53
  9.1 0.7 dynamic_slice.18
  9.8 0.8 fusion.54
  10.7 85.3 %all-gather.3.cloned.1.call-done = bf16[2,3,192,2048]{3,2,1,0:T(8,128)(2,1)} async-done(((bf16[2,3,192,128]{3,2,1,0:T(8,128)(2,1)}), bf16[2,3,192,2048]{3,2,1,0:T(8,128)(2,1)}) %all-gather.3.cloned.1.call-update) | async-done | bytes 4718608 | tf_op jit(solution)/shard_map/all_gather | solution.py:124
  96.0 4.1 fusion.24
  100.1 3.9 fusion.23
  104.0 1.3 fusion.15
  105.3 1.6 fusion.3
  107.5 1.1 fusion.14
  108.6 1.2 fusion.13
  109.8 1.5 fusion.26
  111.4 1.5 fusion.25
  112.9 1.3 fusion.10
  114.2 1.6 fusion.6
  115.8 1.1 fusion.9
  116.9 1.4 fusion.8
  119.3 0.6 maximum_maximum_fusion
  119.9 3.4 copy.26
  123.3 14.0 %reduce-scatter.5.cloned.1.call-done = bf16[8,2,3,192,128]{4,3,2,1,0:T(8,128)(2,1)} async-done(((bf16[16,2,3,192,128]{4,3,2,1,0:T(8,128)(2,1)}), bf16[8,2,3,192,128]{4,3,2,1,0:T(8,128)(2,1)}) %reduce-scatter.5.cloned.1.call-update) | async-done | bytes 2359312 | tf_op jit(solution)/shard_map/reduce_scatter | solution.py:41
  137.4 105.3 %reduce-scatter.7.cloned.1.call-done = bf16[1,2,3,192,128]{4,3,2,1,0:T(8,128)(2,1)} async-done(((bf16[8,2,3,192,128]{4,3,2,1,0:T(8,128)(2,1)}), bf16[1,2,3,192,128]{4,3,2,1,0:T(8,128)(2,1)}) %reduce-scatter.7.cloned.1.call-update) | async-done | bytes 294928 | tf_op jit(solution)/shard_map/reduce_scatter | solution.py:42
  242.7 2.2 fusion.63
  244.9 78.6 %all-gather.5.cloned.1.call-done = bf16[2,3,192,2048]{3,2,1,0:T(8,128)(2,1)} async-done(((bf16[2,3,192,128]{3,2,1,0:T(8,128)(2,1)}), bf16[2,3,192,2048]{3,2,1,0:T(8,128)(2,1)}) %all-gather.5.cloned.1.call-update) | async-done | bytes 4718608 | tf_op jit(solution)/shard_map/all_gather | solution.py:178
  323.5 4.1 fusion.22
  327.7 2.7 fusion.21
  330.3 8.6 %fusion.19 = f32[1024,2048]{1,0:T(8,128)} fusion(bf16[1024,2048]{1,0:T(8,128)(2,1)} %param.23, bf16[2,3,192,2048]{3,2,1,0:T(8,128)(2,1)} %all-gather.5.cloned.1.call-done, f32[192,1024]{1,0:T(8,128)S(1)} %fusion.22, f32[1024]{0:T(1024)S(1)} %bitcast.108), kind=kOutput, calls=%fused_computation.29 | convolution fusion | flops 1611988992 | bytes 14946304 | tf_op jit(solution)/shard_map/dot_general | solution.py:85
  338.9 11.1 %convolution_add_fusion = f32[1024,2048]{1,0:T(8,128)} fusion(f32[1024,2048]{1,0:T(8,128)} %fusion.19, bf16[1024,2048]{1,0:T(8,128)(2,1)} %param.23, bf16[2,3,192,2048]{3,2,1,0:T(8,128)(2,1)} %all-gather.5.cloned.1.call-done, f32[192,1024]{1,0:T(8,128)S(1)} %fusion.21, f32[1024]{0:T(1024)S(1)} %bitcast.107), kind=kOutput, calls=%fused_computation.11 | convolution fusion | flops 1614086144 | bytes 23334912 | tf_op jit(solution)/shard_map/dot_general | solution.py:85
  350.1 0.6 copy-done.7
  350.9 2.1 gather_fusion.4
  353.0 2.2 gather_fusion.2
  355.2 2.2 gather_fusion
  357.4 71.9 %reduce-scatter.9.cloned.1.call-done = f32[1024,512]{1,0:T(8,128)} async-done(((f32[1024,2048]{1,0:T(8,128)}), f32[1024,512]{1,0:T(8,128)}) %reduce-scatter.9.cloned.1.call-update) | async-done | bytes 2097168 | tf_op jit(solution)/shard_map/reduce_scatter | solution.py:48
  429.3 5.3 broadcast_select_fusion
  434.6 32.7 %all_to_all.10 = f32[4,2,3,192,128]{4,3,2,1,0:T(8,128)} all-to-all(f32[4,2,3,192,128]{4,3,2,1,0:T(8,128)S(1)} %bitcast.99), channel_id=1, replica_groups=mesh['dp_0'=2,'dp_1'=4,'dp_2'=2,'slot'=4,'hid'=4] {'slot'}, dimensions={0} | all-to-all | bytes 4718592 | tf_op jit(solution)/shard_map/all_to_all | solution.py:164
  467.3 4.7 all-to-all-start
  472.1 1.7 broadcast_in_dim.64
  473.8 1.0 constant_dynamic-slice_fusion
  474.8 1.7 collective-permute-start
  476.6 2.7 collective-permute-start.1
  479.6 34.0 %collective-permute-done = f32[1,2,3,192,128]{4,3,2,1,0:T(8,128)S(1)} collective-permute-done((f32[1,2,3,192,128]{4,3,2,1,0:T(8,128)S(1)}, f32[1,2,3,192,128]{4,3,2,1,0:T(8,128)S(1)}, u32[]{:S(2)}, u32[]{:S(2)}) %collective-permute-start) | collective-permute-done | bytes 589856 | tf_op jit(solution)/shard_map/ppermute | solution.py:26
  513.6 0.9 constant_dynamic-update-slice_fusion.1
  514.4 11.0 %collective-permute-done.1 = f32[1,2,3,192,128]{4,3,2,1,0:T(8,128)S(1)} collective-permute-done((f32[1,2,3,192,128]{4,3,2,1,0:T(8,128)S(1)}, f32[1,2,3,192,128]{4,3,2,1,0:T(8,128)S(1)}, u32[]{:S(2)}, u32[]{:S(2)}) %collective-permute-start.1) | collective-permute-done | bytes 589856 | tf_op jit(solution)/shard_map/ppermute | solution.py:26
  525.4 0.9 constant_dynamic-update-slice_fusion
  526.3 0.9 constant_dynamic-update-slice_fusion.2
  527.2 2.2 gather_fusion.3
  529.4 2.2 gather_fusion.5
  531.7 2.2 gather_fusion.1
  534.0 1.3 broadcast_select_fusion.3
  535.3 1.8 convert_element_type.66
  (46 shorter events, 2.5 us)
Async XLA Ops:
  7.2 88.8 %all-gather.3.cloned.1.call-start = ((), (), s32[]{:S(2)}) async-start(), calls=%async_computation.6 | async-start | bytes 5013504 | tf_op jit(solution)/shard_map/all_gather | solution.py:124
  9.1 128.2 %reduce-scatter.5.cloned.1.call-start = ((), (), s32[]{:S(2)}) async-start(), calls=%async_computation.7 | async-start | bytes 7077888 | tf_op jit(solution)/shard_map/reduce_scatter | solution.py:41
  96.0 4.1 copy-start.4
  100.1 3.9 copy-start.5
  105.3 2.2 copy-start.6
  123.2 119.5 %copy-start.1 = (f32[2,3,192,128]{3,2,1,0:T(8,128)S(1)}, f32[2,3,192,128]{3,2,1,0:T(8,128)}, u32[]{:S(2)}) copy-start(f32[2,3,192,128]{3,2,1,0:T(8,128)} %param.16) | copy-start | bytes 1769476
  123.2 119.5 %copy-start.2 = (f32[2,3,192,128]{3,2,1,0:T(8,128)S(1)}, f32[2,3,192,128]{3,2,1,0:T(8,128)}, u32[]{:S(2)}) copy-start(f32[2,3,192,128]{3,2,1,0:T(8,128)} %param.17) | copy-start | bytes 1769476
  123.2 119.5 %copy-start.3 = (f32[2,3,192,128]{3,2,1,0:T(8,128)S(1)}, f32[2,3,192,128]{3,2,1,0:T(8,128)}, u32[]{:S(2)}) copy-start(f32[2,3,192,128]{3,2,1,0:T(8,128)} %param.18) | copy-start | bytes 1769476
  123.2 119.4 %reduce-scatter.7.cloned.1.call-start = ((), (), s32[]{:S(2)}) async-start(), calls=%async_computation.8 | async-start | bytes 2654208 | tf_op jit(solution)/shard_map/reduce_scatter | solution.py:42
  137.3 186.2 %all-gather.5.cloned.1.call-start = ((), (), s32[]{:S(2)}) async-start(), calls=%async_computation.9 | async-start | bytes 5013504 | tf_op jit(solution)/shard_map/all_gather | solution.py:178
  244.9 184.4 %reduce-scatter.9.cloned.1.call-start = ((), (), s32[]{:S(2)}) async-start(), calls=%async_computation.10 | async-start | bytes 10485760 | tf_op jit(solution)/shard_map/reduce_scatter | solution.py:48
  323.5 4.1 copy-start
  350.1 0.7 copy-start.7
  350.1 0.7 copy-start.8
  350.1 185.2 %reduce-scatter.11.cloned.1.call-start = ((), (), s32[]{:S(2)}) async-start(), calls=%async_computation.11 | async-start | bytes 2621440 | tf_op jit(solution)/shard_map/reduce_scatter | solution.py:48
  467.3 64.4 %all-to-all-start = ((f32[4,2,3,192,128]{4,3,2,1,0:T(8,128)}), f32[4,2,3,192,128]{4,3,2,1,0:T(8,128)}, u32[]{:S(2)}, u32[]{:S(2)}) async-start(f32[4,2,3,192,128]{4,3,2,1,0:T(8,128)} %bitcast.14), calls=%async_computation.2 | async-start | bytes 4718592 | tf_op jit(solution)/shard_map/all_to_all | solution.py:162
  474.8 38.8 %collective-permute-start = (f32[1,2,3,192,128]{4,3,2,1,0:T(8,128)S(1)}, f32[1,2,3,192,128]{4,3,2,1,0:T(8,128)S(1)}, u32[]{:S(2)}, u32[]{:S(2)}) collective-permute-start(f32[1,2,3,192,128]{4,3,2,1,0:T(8,128)S(1)} %get-tuple-element.18), channel_id=1, source_target_pairs={{0,4},{4,0},{8,12},{12,8},{1,5},{5,1},{9,13},{13,9},{2,6},{6,2},{1... | collective-permute-start | bytes 1769480 | tf_op jit(solution)/shard_map/ppermute | solution.py:26
  476.6 48.9 %collective-permute-start.1 = (f32[1,2,3,192,128]{4,3,2,1,0:T(8,128)S(1)}, f32[1,2,3,192,128]{4,3,2,1,0:T(8,128)S(1)}, u32[]{:S(2)}, u32[]{:S(2)}) collective-permute-start(f32[1,2,3,192,128]{4,3,2,1,0:T(8,128)S(1)} %get-tuple-element.17), channel_id=1, source_target_pairs={{0,8},{4,12},{8,0},{12,4},{1,9},{5,13},{9,1},{13,5},{2,10},{6,14},... | collective-permute-start | bytes 1769480 | tf_op jit(solution)/shard_map/ppermute | solution.py:26
  479.2 47.1 %collective-permute-start.2 = (f32[1,2,3,192,128]{4,3,2,1,0:T(8,128)S(1)}, f32[1,2,3,192,128]{4,3,2,1,0:T(8,128)S(1)}, u32[]{:S(2)}, u32[]{:S(2)}) collective-permute-start(f32[1,2,3,192,128]{4,3,2,1,0:T(8,128)S(1)} %get-tuple-element.16), channel_id=1, source_target_pairs={{0,12},{4,8},{8,4},{12,0},{1,13},{5,9},{9,5},{13,1},{2,14},{6,10},... | collective-permute-start | bytes 1769480 | tf_op jit(solution)/shard_map/ppermute | solution.py:26
Sparse Core Ops, SparseCore 0:
  11.1 84.8 all-gather.2
  123.4 13.8 reduce-scatter.4
  142.0 100.6 reduce-scatter.6
  245.7 77.8 all-gather.4
  350.2 79.0 reduce-scatter.8
  431.7 48.8 reduce-scatter.10
